TPU v7x, 32 devices: a whole 2x2x4 slice. The times are simulated.
32 devices in a mesh: depth: 8 (over z, x), col: 4 (over y, core).
Axes of the slice: x: 2, y: 2, z: 4, core: 2. Of those that a mesh axis runs over, the one named last changes fastest.
Arguments:
- voxel_bins: int32 [32, 128, 2048], P('depth', None, 'col'), may hold values from 0 to 4095
- color_table: bfloat16 [3, 256], replicated, may hold values from 0 to 2
- opacity_table: bfloat16 [256], replicated, may hold values from 0 to 0.125
- brick_order: int32 [8], replicated, may hold values from 0 to 7, as said below
Outputs:
- frame: float32 [4, 16, 8, 2048], P(None, None, 'depth', 'col')
Inputs may be any that keep to these rules, and one draw needn't show every extreme that they name: brick_order is a monotone order of the bricks: either brick_order[b] = b for every b or brick_order[b] = 7 - b for every b.
All inputs are finite; a program needn't handle non-finite values.
Results may differ from a plain program's by a relative error of at most 0.0003.
Values sent between devices are 32-bit elements; how exact they have to be, the bound alone decides.
A program may use at most 192 MiB of HBM per device.

v0:
```python
import jax
import jax.numpy as jnp
from jax import lax
from jax.sharding import PartitionSpec as P

BINS = 256
QUANT_LEVELS = 4096


light_depth = 0.48
light_rows = 0.6
light_cols = 0.64


def with_halo(shard, sides, width):
    for axis, dim in sides:
        devices, length = (lax.axis_size(axis), shard.shape[dim])
        up = [(i, (i + 1) % devices) for i in range(devices - 1)]
        down = [(j, i) for i, j in up]
        last = lax.slice_in_dim(shard, length - width, length, axis=dim)
        first = lax.slice_in_dim(shard, 0, width, axis=dim)
        before = lax.ppermute(last, axis, up)
        after = lax.ppermute(first, axis, down)
        shard = jnp.concatenate([before, shard, after], axis=dim)
    return shard


def from_partner(shard, axis, distance):
    return lax.ppermute(shard, axis, [(i, i ^ 1 << distance) for i in range(lax.axis_size(axis))])


def part_of(field, start, stop, dimension):
    return lax.slice_in_dim(field, start, stop, axis=dimension)


def smooth_valid(field, dimension):
    length = field.shape[dimension]
    return (
        part_of(field, 0, length - 2, dimension)
        + 2.0 * part_of(field, 1, length - 1, dimension)
        + part_of(field, 2, length, dimension)
    )


def differ_valid(field, dimension):
    length = field.shape[dimension]
    return part_of(field, 2, length, dimension) - part_of(field, 0, length - 2, dimension)


def shifted(field, dimension, offset):
    length = field.shape[dimension]
    zero_shape = list(field.shape)
    zero_shape[dimension] = 1
    zero_rows = jnp.zeros(zero_shape, field.dtype)
    if offset > 0:
        return jnp.concatenate(
            [zero_rows, part_of(field, 0, length - 1, dimension)], axis=dimension
        )
    return jnp.concatenate([part_of(field, 1, length, dimension), zero_rows], axis=dimension)


def smooth_same(field, dimension):
    return shifted(field, dimension, 1) + 2.0 * field + shifted(field, dimension, -1)


def differ_same(field, dimension):
    return shifted(field, dimension, -1) - shifted(field, dimension, 1)


def gradient(padded):
    grad_depth = smooth_valid(smooth_same(differ_valid(padded, 0), 1), 2)
    grad_rows = smooth_valid(smooth_valid(differ_same(padded, 1), 0), 2)
    grad_cols = smooth_same(smooth_valid(differ_valid(padded, 2), 0), 1)
    return (grad_depth, grad_rows, grad_cols)


def build_table(color_table, opacity_table):
    lower_table = jnp.concatenate([color_table, opacity_table[None, :]], axis=0)
    upper_table = jnp.concatenate([lower_table[:, 1:], lower_table[:, -1:]], axis=1)
    return jnp.concatenate([lower_table, upper_table], axis=0)


def samples_of(bins_block, grad_depth, grad_rows, grad_cols, table_pairs):
    levels = QUANT_LEVELS - 1
    scaled = bins_block * (BINS - 1)
    lower_bin = scaled // levels
    fraction = (scaled - lower_bin * levels).astype(jnp.float32) / float(levels)
    values = jnp.take(table_pairs, lower_bin, axis=1).astype(jnp.float32)
    interpolated = values[:4] * (1.0 - fraction) + values[4:] * fraction
    facing = light_depth * grad_depth + light_rows * grad_rows + light_cols * grad_cols
    magnitude = grad_depth * grad_depth + grad_rows * grad_rows + grad_cols * grad_cols
    shading = 0.2 + 0.8 * jnp.abs(facing) / jnp.sqrt(magnitude + 1.0)
    opacity = interpolated[3]
    colour = interpolated[:3] * (shading * opacity)[None]
    return jnp.concatenate([colour, opacity[None]], axis=0)


def over_blend(front_part, back_part):
    return front_part + (1.0 - front_part[3:4]) * back_part


def body(voxel_bins, color_table, opacity_table, brick_order):
    density = voxel_bins.astype(jnp.float32) / float(QUANT_LEVELS - 1)
    padded = with_halo(density, (("depth", 0), ("col", 2)), 1)
    grad_depth, grad_rows, grad_cols = gradient(padded)
    table_pairs = build_table(color_table, opacity_table)
    samples = samples_of(voxel_bins, grad_depth, grad_rows, grad_cols, table_pairs)
    ascending = brick_order[0] < brick_order[brick_order.shape[0] - 1]
    slab_count = voxel_bins.shape[0]
    band_rows = voxel_bins.shape[1]
    tile_cols = voxel_bins.shape[2]
    picture = jnp.zeros((4, band_rows, tile_cols), jnp.float32)
    for slab_pos in range(slab_count):
        front_slice = jnp.where(
            ascending, samples[:, slab_pos], samples[:, slab_count - 1 - slab_pos]
        )
        picture = picture + (1.0 - picture[3:4]) * front_slice
    brick_count = lax.axis_size("depth")
    brick_index = lax.axis_index("depth")
    rounds = brick_count.bit_length() - 1
    for bit_pos in range(rounds):
        current_rows = picture.shape[1]
        halves = picture.reshape(4, current_rows // 2, 2, tile_cols)
        even_rows = halves[:, :, 0]
        odd_rows = halves[:, :, 1]
        my_bit = brick_index // 2**bit_pos % 2
        kept_rows = jnp.where(my_bit == 0, even_rows, odd_rows)
        sent_rows = jnp.where(my_bit == 0, odd_rows, even_rows)
        partner_rows = from_partner(sent_rows, "depth", bit_pos)
        mine_front = (my_bit == 0) == ascending
        picture = jnp.where(
            mine_front, over_blend(kept_rows, partner_rows), over_blend(partner_rows, kept_rows)
        )
    frame_tile = picture[:, :, None, :]
    return frame_tile


def solution(mesh):
    in_specs = (P("depth", None, "col"), P(), P(), P())
    out_specs = P(None, None, "depth", "col")
    return jax.shard_map(body, mesh=mesh, in_specs=in_specs, out_specs=out_specs, check_vma=False)
```

profile of v0, /device:TPU:28, one launch (start us, length us, event | category | flops | bytes accessed | tf_op | source)
XLA Modules:
  0.0 1127.0 jit_solution(4509956502366599251)
XLA Ops:
  0.0 2.7 broadcast_subtract_fusion
  3.5 3.3 collective-permute-start.1
  6.8 2.6 collective-permute-start
  9.4 2.2 compare_and_fusion
  11.9 1.5 copy.161
  14.5 990.2 %gather_fusion = bf16[262144,8]{1,0:T(8,128)(2,1)} fusion(bf16[8,256]{0,1:T(8,128)(2,1)S(1)} %copy.118, s32[262144]{0:T(1024)} %broadcast_clamp_fusion), kind=kCustom, calls=%fused_computation | custom fusion | bytes 9437184 | tf_op jit(solution)/shard_map/jit(_take)/gather | solution.py:88
  1004.8 54.2 %copy.119 = bf16[4,128,512,8]{2,1,0,3:T(8,128)(2,1)} copy(bf16[4,128,512,8]{3,2,1,0:T(8,128)(2,1)} %bitcast.1) | data formatting | bytes 8388608 | tf_op jit(solution)/shard_map/jit(_take)/gather | solution.py:88
  1059.0 3.1 convert_bitcast_fusion
  1062.1 3.4 fusion
  1065.5 1.9 pad_maximum_fusion.8
  1067.4 1.9 collective-permute-start.2
  1069.3 3.8 collective-permute-start.3
  1073.7 1.3 slice.252
  1076.7 1.9 collective-permute-done.3
  1078.5 1.6 pad_maximum_fusion
  1080.6 2.0 fusion.1
  1083.9 1.5 copy-done
  1088.2 1.7 copy.135
  1090.6 1.6 copy.132
  1092.2 1.7 copy.126
  1095.3 3.9 fusion.16
  1099.6 10.3 collective-permute-done.4
  1111.8 6.5 collective-permute-done.5
  1119.4 6.6 collective-permute-done.6
  (66 shorter events, 13.8 us)
Async XLA Ops:
  0.0 9.4 copy-start.1
  2.7 9.0 copy-start.5
  2.7 9.0 copy-start.3
  3.5 1062.0 %collective-permute-start.1 = (f32[1,128,512]{2,1,0:T(8,128)}, f32[1,128,512]{2,1,0:T(8,128)S(1)}, u32[]{:S(2)}, u32[]{:S(2)}) collective-permute-start(f32[1,128,512]{2,1,0:T(8,128)} %get-tuple-element.27), channel_id=1, source_target_pairs={{4,0},{8,4},{12,8},{16,12},{20,16},{24,20},{28,24},{5,1},{9,5},{13... | collective-permute-start | bytes 786440 | tf_op jit(solution)/shard_map/ppermute | solution.py:23
  6.8 1058.7 %collective-permute-start = (f32[1,128,512]{2,1,0:T(8,128)}, f32[1,128,512]{2,1,0:T(8,128)}, u32[]{:S(2)}, u32[]{:S(2)}) collective-permute-start(f32[1,128,512]{2,1,0:T(8,128)} %get-tuple-element.26), channel_id=1, source_target_pairs={{0,4},{4,8},{8,12},{12,16},{16,20},{20,24},{24,28},{1,5},{5,9},{9,... | collective-permute-start | bytes 786440 | tf_op jit(solution)/shard_map/ppermute | solution.py:22
  1065.5 7.6 copy-start.4
  1067.4 9.3 collective-permute-start.2
  1069.3 9.2 collective-permute-start.3
  1083.2 2.2 copy-start
  1093.9 1.4 copy-start.2
  1099.3 10.5 collective-permute-start.4
  1110.5 7.8 collective-permute-start.5
  1118.7 7.3 collective-permute-start.6
where the time goes:
time: 1150 us; the launch traced here: 1130 us
  local copies, waits for them, and re-layouts  1060 us (92%)
  other arithmetic  26.9 us (2%)
  waiting for transfers between devices  25.5 us (2%)
  starting transfers between devices  13.5 us (1%)
    gather x2, local copies, waits for them, and re-layouts, samples_of(): values = jnp.take(table_pairs, lower_bin, axis=1).astype(jnp.float32)  1040 us
    ppermute x3, waiting for transfers between devices, from_partner(): lax.ppermute(shard, axis, [(i, i ^ 1 << distance) for i in range(lax.axis...  23.4 us
  transfers between devices with their start and end apart: 7, of which 5 were waited for; matrix products, arithmetic and copies ran while one was open for 94% of the time, Pallas kernels for 0%

commit v1 on v0

v1 whole, which is shorter than its diff:
```python
import functools

import jax
import jax.numpy as jnp
from jax import lax
from jax.experimental import pallas as pl
from jax.experimental.pallas import tpu as pltpu
from jax.sharding import PartitionSpec as P

BINS = 256
LEVELS = 4095.0
LIGHT = (0.48, 0.6, 0.64)
GROUP = 8


def planes(v_ref, k, c):
    lo, mid, hi = v_ref[k, c], v_ref[k, c + 1], v_ref[k, c + 2]
    width = lo.shape[-1]
    cols = width - 128
    smooth = lo + 2.0 * mid + hi
    differ = hi - lo
    s_left, s_right = pltpu.roll(smooth, 1, 1)[:, :cols], pltpu.roll(smooth, width - 1, 1)[:, :cols]
    d_left, d_right = pltpu.roll(differ, 1, 1)[:, :cols], pltpu.roll(differ, width - 1, 1)[:, :cols]
    a = s_left + 2.0 * smooth[:, :cols] + s_right
    b = d_left + 2.0 * differ[:, :cols] + d_right
    g = s_right - s_left
    return a, b, g


def lookup(tables, voxels):
    outs = [[] for _ in range(4)]
    for j in range(voxels.shape[1] // 128):
        v = voxels[:, j * 128 : (j + 1) * 128]
        scaled = v * 17.0
        lower = jnp.floor((scaled + 0.5) * (1.0 / 273.0))
        fraction = (scaled - lower * 273.0) * (1.0 / 273.0)
        index = lower.astype(jnp.int32)
        high = index >= 128
        lane = jnp.bitwise_and(index, 127)
        for q in range(4):
            base = jnp.where(
                high,
                jnp.take_along_axis(tables[q][1], lane, axis=1),
                jnp.take_along_axis(tables[q][0], lane, axis=1),
            )
            step = jnp.where(
                high,
                jnp.take_along_axis(tables[q + 4][1], lane, axis=1),
                jnp.take_along_axis(tables[q + 4][0], lane, axis=1),
            )
            outs[q].append(base + fraction * step)
    return [jnp.concatenate(o, axis=1) for o in outs]


def load_tables(tab_ref):
    return [
        [jnp.broadcast_to(tab_ref[q : q + 1, h * 128 : (h + 1) * 128], (8, 128)) for h in range(2)]
        for q in range(8)
    ]


def composite_tile(v_ref, tab_ref, c, slices):
    tables = load_tables(tab_ref)
    cols = v_ref.shape[-1] - 128
    ascending = jnp.broadcast_to(tab_ref[8:9, 0:1], (8, cols)) > 0.5
    before = planes(v_ref, 0, c)
    here = planes(v_ref, 1, c)
    acc = [jnp.zeros((8, cols), jnp.float32)] * 4
    for k in range(1, slices + 1):
        after = planes(v_ref, k + 1, c)
        gd = after[0] - before[0]
        gr = before[1] + 2.0 * here[1] + after[1]
        gc = before[2] + 2.0 * here[2] + after[2]
        facing = LIGHT[0] * gd + LIGHT[1] * gr + LIGHT[2] * gc
        magnitude = gd * gd + gr * gr + gc * gc
        shading = 0.2 + 0.8 * jnp.abs(facing) * lax.rsqrt(magnitude + LEVELS * LEVELS)
        red, green, blue, opacity = lookup(tables, v_ref[k, c + 1][:, :cols])
        weight = shading * opacity
        new = [red * weight, green * weight, blue * weight, opacity]
        trans = 1.0 - jnp.where(ascending, acc[3], opacity)
        acc = [
            jnp.where(ascending, a, n) + trans * jnp.where(ascending, n, a)
            for a, n in zip(acc, new)
        ]
        before, here = here, after
    return acc


def local_kernel(slices, v_ref, tab_ref, out_ref):
    def step(c, carry):
        acc = composite_tile(v_ref, tab_ref, c, slices)
        for q in range(4):
            out_ref[c, q] = acc[q]
        return carry

    lax.fori_loop(0, GROUP, step, 0)


def build_tables(color_table, opacity_table, brick_order):
    lower = jnp.concatenate([color_table, opacity_table[None]], axis=0).astype(jnp.float32)
    upper = jnp.concatenate([lower[:, 1:], lower[:, -1:]], axis=1)
    asc = (brick_order[0] < brick_order[-1]).astype(jnp.float32)
    return jnp.concatenate(
        [lower, upper - lower, jnp.full((8, BINS), asc, jnp.float32)], axis=0
    )


def shift_perm(axis, distance):
    n = lax.axis_size(axis)
    return [(i, i + distance) for i in range(n) if 0 <= i + distance < n]


def swap(x, bit):
    return lax.ppermute(x, "depth", [(i, i ^ bit) for i in range(lax.axis_size("depth"))])


def over(front, back, axis):
    alpha = lax.slice_in_dim(front, 3, 4, axis=axis)
    return front + (1.0 - alpha) * back


def body(voxel_bins, color_table, opacity_table, brick_order):
    me = lax.axis_index("depth")
    n = lax.axis_size("depth")
    odd = me % 2 == 1
    slices, rows, cols = voxel_bins.shape
    half = rows // 2
    tiles = half // GROUP
    v = voxel_bins.astype(jnp.float32)
    zero = jnp.zeros((slices, 1, cols), jnp.float32)
    top = jnp.concatenate([zero, v[:, : half + 1]], axis=1)
    bottom = jnp.concatenate([v[:, half - 1 :], zero], axis=1)
    mine = jnp.where(odd, bottom, top)
    theirs = swap(jnp.where(odd, top, bottom), 1)
    pair = jnp.concatenate([jnp.where(odd, theirs, mine), jnp.where(odd, mine, theirs)], axis=0)
    from_before = lax.ppermute(pair[-1:], "depth", shift_perm("depth", 2))
    from_after = lax.ppermute(pair[:1], "depth", shift_perm("depth", -2))
    pair = jnp.concatenate([from_before, pair, from_after], axis=0)
    from_left = lax.ppermute(pair[:, :, -128:], "col", shift_perm("col", 1))
    from_right = lax.ppermute(pair[:, :, :128], "col", shift_perm("col", -1))
    edge = jnp.where(jnp.arange(128) < 64, from_right, from_left)
    pair = jnp.concatenate([pair, edge], axis=2)
    ext = jnp.stack(
        [pair[:, c : c + 8 * (tiles - 1) + 1 : 8] for c in range(GROUP + 2)], axis=1
    )
    tab = build_tables(color_table, opacity_table, brick_order)
    part = pl.pallas_call(
        functools.partial(local_kernel, 2 * slices),
        out_shape=jax.ShapeDtypeStruct((GROUP, 4, tiles, cols), jnp.float32),
        in_specs=[pl.BlockSpec(memory_space=pltpu.VMEM)] * 2,
        out_specs=pl.BlockSpec(memory_space=pltpu.VMEM),
        compiler_params=pltpu.CompilerParams(vmem_limit_bytes=40 * 2**20),
    )(ext, tab)
    ascending = brick_order[0] < brick_order[-1]
    part = part.reshape(2, 2, 2, 4, tiles, cols)
    for axis, bit in ((1, 2), (0, 4)):
        set_bit = me // bit % 2 == 1
        first, second = jnp.take(part, 0, axis=axis), jnp.take(part, 1, axis=axis)
        part = jnp.expand_dims(jnp.where(set_bit, second, first), axis)
        got = jnp.expand_dims(swap(jnp.where(set_bit, first, second), bit), axis)
        front = set_bit != ascending
        part = jnp.where(front, over(part, got, 3), over(got, part, 3))
    part = part.reshape(2, 4, tiles, cols)
    keep = jnp.where(odd, part[1], part[0])
    got = swap(jnp.where(odd, part[0], part[1]), 1)
    picture = jnp.where(
        odd, jnp.concatenate([got, keep], axis=1), jnp.concatenate([keep, got], axis=1)
    )
    return finish(picture, ascending, me, n)


def finish(picture, ascending, me, n):
    bit = GROUP
    while bit < n:
        count = picture.shape[1]
        halves = picture.reshape(4, count // 2, 2, picture.shape[2])
        set_bit = me // bit % 2 == 1
        keep = jnp.where(set_bit, halves[:, :, 1], halves[:, :, 0])
        got = swap(jnp.where(set_bit, halves[:, :, 0], halves[:, :, 1]), bit)
        picture = jnp.where(set_bit != ascending, over(keep, got, 0), over(got, keep, 0))
        bit *= 2
    return picture[:, :, None, :]


def solution(mesh):
    in_specs = (P("depth", None, "col"), P(), P(), P())
    out_specs = P(None, None, "depth", "col")
    return jax.shard_map(body, mesh=mesh, in_specs=in_specs, out_specs=out_specs, check_vma=False)
```

time: 1150 us -> 72.1 us (0.06); the launches traced: 1130 us -> 71.8 us
  local copies, waits for them, and re-layouts: 1060 us -> 7.15 us
  other arithmetic: 26.9 us -> 4.44 us
  waiting for transfers between devices: 25.5 us -> 37.7 us
    gather x2 -> x0, local copies, waits for them, and re-layouts: 1040 us -> none  [samples_of(): values = jnp.take(table_pairs, lower_bin, axis=1).astype(jnp.float32)]
    ppermute x7 -> x8, waiting for transfers between devices: 25.5 us -> 37.7 us  [the longest x4 29.3 us: swap(): lax.ppermute(x, 'depth', [(i, i ^ bit) for i in range(lax.axis_size('dept...]
  transfers between devices with their start and end apart: 7 -> 8, of which waited for: 5 -> 8; matrix products, arithmetic and copies ran while one was open for 94% -> 1% of each run, Pallas kernels for 0% -> 0%
where the time goes in v1:
time: 72.1 us; the launch traced here: 71.8 us
  waiting for transfers between devices  37.7 us (52%)
  starting transfers between devices  13.2 us (18%)
  Pallas kernels  7.6 us (11%)
  local copies, waits for them, and re-layouts  7.15 us (10%)
  other arithmetic  4.44 us (6%)
  between operations  1.76 us (2%)
    ppermute x4, waiting for transfers between devices, swap(): lax.ppermute(x, 'depth', [(i, i ^ bit) for i in range(lax.axis_size('dept...  29.3 us
    pallas_call x1, Pallas kernels, body(): pl.pallas_call(functools.partial(local_kernel, 2 * slices), out_shape=jax...  7.6 us
    ppermute x1, waiting for transfers between devices, body(): from_before = lax.ppermute(pair[-1:], 'depth', shift_perm('depth', 2))  4.39 us
    ppermute x4, starting transfers between devices, swap(): lax.ppermute(x, 'depth', [(i, i ^ bit) for i in range(lax.axis_size('dept...  3.94 us
    slice x10, local copies, waits for them, and re-layouts, body(): pair[:, c:c + 8 * (tiles - 1) + 1:8]  3.67 us
    ppermute x1, starting transfers between devices, body(): from_right = lax.ppermute(pair[:, :, :128], 'col', shift_perm('col', -1))  3.64 us
    ppermute x1, starting transfers between devices, body(): from_after = lax.ppermute(pair[:1], 'depth', shift_perm('depth', -2))  2.36 us
    unnamed x18, local copies, waits for them, and re-layouts  2.04 us
  transfers between devices with their start and end apart: 8, of which 8 were waited for; matrix products, arithmetic and copies ran while one was open for 1% of the time, Pallas kernels for 0%

profile of v1, /device:TPU:28, one launch (start us, length us, event | category | flops | bytes accessed | tf_op | source)
XLA Modules:
  0.0 71.8 jit_solution(7740285702682175778)
XLA Ops:
  0.0 1.3 %convert_element_type.9 = f32[4,128,512]{2,1,0:T(8,128)S(1)} convert(s32[4,128,512]{2,1,0:T(8,128)} %param.12) | non-fusion elementwise | flops 262144 | bytes 2097152 | tf_op jit(solution)/shard_map/convert_element_type | solution.py:129
  2.0 1.6 %collective-permute-start = (f32[4,66,512]{2,0,1:T(4,128)S(1)}, f32[4,66,512]{2,0,1:T(4,128)S(1)}, u32[]{:S(2)}, u32[]{:S(2)}) collective-permute-start(f32[4,66,512]{2,0,1:T(4,128)S(1)} %copy.16), channel_id=1, source_target_pairs={{0,4},{4,0},{8,12},{12,8},{16,20},{20,16},{24,28},{28,24},{1,5},{5... | collective-permute-start | bytes 1622024 | tf_op jit(solution)/shard_map/ppermute | solution.py:114
  3.6 12.5 %collective-permute-done = f32[4,66,512]{2,0,1:T(4,128)S(1)} collective-permute-done((f32[4,66,512]{2,0,1:T(4,128)S(1)}, f32[4,66,512]{2,0,1:T(4,128)S(1)}, u32[]{:S(2)}, u32[]{:S(2)}) %collective-permute-start) | collective-permute-done | bytes 540704 | tf_op jit(solution)/shard_map/ppermute | solution.py:114
  16.4 2.4 %collective-permute-start.2 = (f32[1,66,512]{2,1,0:T(8,128)S(1)}, f32[1,66,512]{2,1,0:T(8,128)S(1)}, u32[]{:S(2)}, u32[]{:S(2)}) collective-permute-start(f32[1,66,512]{2,1,0:T(8,128)S(1)} %slice.181), channel_id=1, source_target_pairs={{8,0},{12,4},{16,8},{20,12},{24,16},{28,20},{9,1},{13,5},{17,9},{2... | collective-permute-start | bytes 405512 | tf_op jit(solution)/shard_map/ppermute | solution.py:137
  18.8 1.3 %collective-permute-start.1 = (f32[1,66,512]{2,1,0:T(8,128)S(1)}, f32[1,66,512]{2,1,0:T(8,128)S(1)}, u32[]{:S(2)}, u32[]{:S(2)}) collective-permute-start(f32[1,66,512]{2,1,0:T(8,128)S(1)} %slice.180), channel_id=1, source_target_pairs={{0,8},{4,12},{8,16},{12,20},{16,24},{20,28},{1,9},{5,13},{9,17},{1... | collective-permute-start | bytes 405512 | tf_op jit(solution)/shard_map/ppermute | solution.py:136
  20.1 0.6 fusion.7
  20.7 0.7 %collective-permute-done.2 = f32[1,66,512]{2,1,0:T(8,128)S(1)} collective-permute-done((f32[1,66,512]{2,1,0:T(8,128)S(1)}, f32[1,66,512]{2,1,0:T(8,128)S(1)}, u32[]{:S(2)}, u32[]{:S(2)}) %collective-permute-start.2) | collective-permute-done | bytes 135200 | tf_op jit(solution)/shard_map/ppermute | solution.py:137
  21.4 4.4 %collective-permute-done.1 = f32[1,66,512]{2,1,0:T(8,128)S(1)} collective-permute-done((f32[1,66,512]{2,1,0:T(8,128)S(1)}, f32[1,66,512]{2,1,0:T(8,128)S(1)}, u32[]{:S(2)}, u32[]{:S(2)}) %collective-permute-start.1) | collective-permute-done | bytes 135200 | tf_op jit(solution)/shard_map/ppermute | solution.py:136
  25.9 1.9 %collective-permute-start.4 = (f32[10,66,128]{2,1,0:T(8,128)S(1)}, f32[10,66,128]{2,1,0:T(8,128)S(1)}, u32[]{:S(2)}, u32[]{:S(2)}) collective-permute-start(f32[10,66,128]{2,1,0:T(8,128)S(1)} %get-tuple-element.55), channel_id=1, source_target_pairs={{0,1},{1,2},{2,3},{4,5},{5,6},{6,7},{8,9},{9,10},{10,11},{12,13},{... | collective-permute-start | bytes 1013768 | tf_op jit(solution)/shard_map/ppermute | solution.py:139
  27.8 3.6 %collective-permute-start.3 = (f32[10,66,128]{2,1,0:T(8,128)S(1)}, f32[10,66,128]{2,1,0:T(8,128)S(1)}, u32[]{:S(2)}, u32[]{:S(2)}) collective-permute-start(f32[10,66,128]{2,1,0:T(8,128)S(1)} %get-tuple-element.56), channel_id=1, source_target_pairs={{1,0},{2,1},{3,2},{5,4},{6,5},{7,6},{9,8},{10,9},{11,10},{13,12},{... | collective-permute-start | bytes 1013768 | tf_op jit(solution)/shard_map/ppermute | solution.py:140
  33.2 1.5 %collective-permute-done.4 = f32[10,66,128]{2,1,0:T(8,128)S(1)} collective-permute-done((f32[10,66,128]{2,1,0:T(8,128)S(1)}, f32[10,66,128]{2,1,0:T(8,128)S(1)}, u32[]{:S(2)}, u32[]{:S(2)}) %collective-permute-start.4) | collective-permute-done | bytes 337952 | tf_op jit(solution)/shard_map/ppermute | solution.py:139
  34.7 1.8 %collective-permute-done.3 = f32[10,66,128]{2,1,0:T(8,128)S(1)} collective-permute-done((f32[10,66,128]{2,1,0:T(8,128)S(1)}, f32[10,66,128]{2,1,0:T(8,128)S(1)}, u32[]{:S(2)}, u32[]{:S(2)}) %collective-permute-start.3) | collective-permute-done | bytes 337952 | tf_op jit(solution)/shard_map/ppermute | solution.py:140
  38.7 0.9 %slice.93 = f32[10,8,640]{2,1,0:T(8,128)} slice(f32[10,66,640]{2,1,0:T(8,128)S(1)} %pad_maximum_fusion), slice={[0:10:1], [1:58:8], [0:640:1]} | slice | bytes 409600 | tf_op jit(solution)/shard_map/slice | solution.py:144
  39.5 0.8 %slice.92 = f32[10,8,640]{2,1,0:T(8,128)} slice(f32[10,66,640]{2,1,0:T(8,128)S(1)} %pad_maximum_fusion), slice={[0:10:1], [0:57:8], [0:640:1]} | slice | bytes 409600 | tf_op jit(solution)/shard_map/slice | solution.py:144
  40.4 0.9 %bitcast_dynamic-update-slice_fusion.8 = f32[10,10,8,640]{3,2,1,0:T(8,128)S(1)} fusion(f32[10,8,640]{2,1,0:T(8,128)} %slice.92), kind=kLoop, calls=%fused_computation.26 | loop fusion | bytes 409600
  41.3 0.9 %bitcast_dynamic-update-slice_fusion.7 = f32[10,10,8,640]{3,2,1,0:T(8,128)S(1)} fusion(f32[10,10,8,640]{3,2,1,0:T(8,128)S(1)} %bitcast_dynamic-update-slice_fusion.8, f32[10,8,640]{2,1,0:T(8,128)} %slice.93), kind=kLoop, calls=%fused_computation.25 | loop fusion | bytes 409600
  42.5 7.6 %shard_map.46 = f32[8,4,8,512]{3,2,1,0:T(8,128)S(1)} custom-call(f32[10,10,8,640]{3,2,1,0:T(8,128)S(1)} %bitcast_dynamic-update-slice_fusion.9.v_ref, f32[16,256]{1,0:T(8,128)S(1)} %maximum_maximum_fusion.tab_ref), custom_call_target="tpu_custom_call" | custom-call | tf_op jit(solution)/shard_map/pallas_call | solution.py:147
  50.6 0.5 collective-permute-start.5
  51.1 7.1 %collective-permute-done.5 = f32[2,2,4,8,512]{4,0,3,2,1:T(2,128)S(1)} collective-permute-done((f32[2,2,4,8,512]{4,0,3,2,1:T(2,128)S(1)}, f32[2,2,4,8,512]{4,0,3,2,1:T(2,128)S(1)}, u32[]{:S(2)}, u32[]{:S(2)}) %collective-permute-start.5) | collective-permute-done | bytes 262176 | tf_op jit(solution)/shard_map/ppermute | solution.py:114
  58.2 0.5 select_bitcast_fusion
  59.3 7.0 %collective-permute-done.6 = f32[1,2,4,8,512]{4,0,3,2,1:T(1,128)S(1)} collective-permute-done((f32[1,2,4,8,512]{4,0,3,2,1:T(1,128)S(1)}, f32[1,2,4,8,512]{4,0,3,2,1:T(1,128)S(1)}, u32[]{:S(2)}, u32[]{:S(2)}) %collective-permute-start.6) | collective-permute-done | bytes 131104 | tf_op jit(solution)/shard_map/ppermute | solution.py:114
  66.6 1.6 %collective-permute-start.7 = (f32[4,8,512]{2,1,0:T(8,128)S(1)}, f32[4,8,512]{2,1,0:T(8,128)S(1)}, u32[]{:S(2)}, u32[]{:S(2)}) collective-permute-start(f32[4,8,512]{2,1,0:T(8,128)S(1)} %bitcast.101), channel_id=1, source_target_pairs={{0,4},{4,0},{8,12},{12,8},{16,20},{20,16},{24,28},{28,24},{1,5},{5... | collective-permute-start | bytes 196616 | tf_op jit(solution)/shard_map/ppermute | solution.py:114
  68.2 2.8 %collective-permute-done.7 = f32[4,8,512]{2,1,0:T(8,128)S(1)} collective-permute-done((f32[4,8,512]{2,1,0:T(8,128)S(1)}, f32[4,8,512]{2,1,0:T(8,128)S(1)}, u32[]{:S(2)}, u32[]{:S(2)}) %collective-permute-start.7) | collective-permute-done | bytes 65568 | tf_op jit(solution)/shard_map/ppermute | solution.py:114
  71.0 0.8 %broadcast_select_fusion.5 = f32[4,16,1,512]{3,2,1,0:T(1,128)} fusion(pred[]{:T(512)S(6)} %eq.13, f32[4,8,1,512]{3,2,1,0:T(1,128)S(1)} %get-tuple-element.66, f32[4,8,1,512]{3,2,1,0:T(1,128)S(1)} %concatenate.52), kind=kLoop, calls=%fused_computation.17 | loop fusion | flops 98304 | bytes 262145 | tf_op jit(solution)/shard_map/jit(_where)/select_n | solution.py:166
  (54 shorter events, 5.2 us)
Async XLA Ops:
  1.3 2.2 %copy-start.2 = (bf16[256]{0:T(256)(128)(2,1)S(1)}, bf16[256]{0:T(256)(128)(2,1)}, u32[]{:S(2)}) copy-start(bf16[256]{0:T(256)(128)(2,1)} %param.14) | copy-start | bytes 1540
  1.3 2.2 %copy-start = (bf16[3,256]{1,0:T(4,128)(2,1)S(1)}, bf16[3,256]{1,0:T(4,128)(2,1)}, u32[]{:S(2)}) copy-start(bf16[3,256]{1,0:T(4,128)(2,1)} %param.13) | copy-start | bytes 4612
  1.6 18.5 %copy-start.1 = (s32[8]{0:T(128)S(1)}, s32[8]{0:T(128)}, u32[]{:S(2)}) copy-start(s32[8]{0:T(128)} %param.15) | copy-start | bytes 100
  2.0 14.1 %collective-permute-start = (f32[4,66,512]{2,0,1:T(4,128)S(1)}, f32[4,66,512]{2,0,1:T(4,128)S(1)}, u32[]{:S(2)}, u32[]{:S(2)}) collective-permute-start(f32[4,66,512]{2,0,1:T(4,128)S(1)} %copy.16), channel_id=1, source_target_pairs={{0,4},{4,0},{8,12},{12,8},{16,20},{20,16},{24,28},{28,24},{1,5},{5... | collective-permute-start | bytes 1622024 | tf_op jit(solution)/shard_map/ppermute | solution.py:114
  16.4 5.0 %collective-permute-start.2 = (f32[1,66,512]{2,1,0:T(8,128)S(1)}, f32[1,66,512]{2,1,0:T(8,128)S(1)}, u32[]{:S(2)}, u32[]{:S(2)}) collective-permute-start(f32[1,66,512]{2,1,0:T(8,128)S(1)} %slice.181), channel_id=1, source_target_pairs={{8,0},{12,4},{16,8},{20,12},{24,16},{28,20},{9,1},{13,5},{17,9},{2... | collective-permute-start | bytes 405512 | tf_op jit(solution)/shard_map/ppermute | solution.py:137
  18.8 7.0 %collective-permute-start.1 = (f32[1,66,512]{2,1,0:T(8,128)S(1)}, f32[1,66,512]{2,1,0:T(8,128)S(1)}, u32[]{:S(2)}, u32[]{:S(2)}) collective-permute-start(f32[1,66,512]{2,1,0:T(8,128)S(1)} %slice.180), channel_id=1, source_target_pairs={{0,8},{4,12},{8,16},{12,20},{16,24},{20,28},{1,9},{5,13},{9,17},{1... | collective-permute-start | bytes 405512 | tf_op jit(solution)/shard_map/ppermute | solution.py:136
  25.9 8.8 %collective-permute-start.4 = (f32[10,66,128]{2,1,0:T(8,128)S(1)}, f32[10,66,128]{2,1,0:T(8,128)S(1)}, u32[]{:S(2)}, u32[]{:S(2)}) collective-permute-start(f32[10,66,128]{2,1,0:T(8,128)S(1)} %get-tuple-element.55), channel_id=1, source_target_pairs={{0,1},{1,2},{2,3},{4,5},{5,6},{6,7},{8,9},{9,10},{10,11},{12,13},{... | collective-permute-start | bytes 1013768 | tf_op jit(solution)/shard_map/ppermute | solution.py:139
  27.8 8.7 %collective-permute-start.3 = (f32[10,66,128]{2,1,0:T(8,128)S(1)}, f32[10,66,128]{2,1,0:T(8,128)S(1)}, u32[]{:S(2)}, u32[]{:S(2)}) collective-permute-start(f32[10,66,128]{2,1,0:T(8,128)S(1)} %get-tuple-element.56), channel_id=1, source_target_pairs={{1,0},{2,1},{3,2},{5,4},{6,5},{7,6},{9,8},{10,9},{11,10},{13,12},{... | collective-permute-start | bytes 1013768 | tf_op jit(solution)/shard_map/ppermute | solution.py:140
  50.6 7.6 %collective-permute-start.5 = (f32[2,2,4,8,512]{4,0,3,2,1:T(2,128)S(1)}, f32[2,2,4,8,512]{4,0,3,2,1:T(2,128)S(1)}, u32[]{:S(2)}, u32[]{:S(2)}) collective-permute-start(f32[2,2,4,8,512]{4,0,3,2,1:T(2,128)S(1)} %get-tuple-element.60), channel_id=1, source_target_pairs={{0,8},{4,12},{8,0},{12,4},{16,24},{20,28},{24,16},{28,20},{1,9},{5... | collective-permute-start | bytes 786440 | tf_op jit(solution)/shard_map/ppermute | solution.py:114
  58.9 7.3 %collective-permute-start.6 = (f32[1,2,4,8,512]{4,0,3,2,1:T(1,128)S(1)}, f32[1,2,4,8,512]{4,0,3,2,1:T(1,128)S(1)}, u32[]{:S(2)}, u32[]{:S(2)}) collective-permute-start(f32[1,2,4,8,512]{4,0,3,2,1:T(1,128)S(1)} %get-tuple-element.63), channel_id=1, source_target_pairs={{0,16},{4,20},{8,24},{12,28},{16,0},{20,4},{24,8},{28,12},{1,17},{... | collective-permute-start | bytes 393224 | tf_op jit(solution)/shard_map/ppermute | solution.py:114
  66.6 4.3 %collective-permute-start.7 = (f32[4,8,512]{2,1,0:T(8,128)S(1)}, f32[4,8,512]{2,1,0:T(8,128)S(1)}, u32[]{:S(2)}, u32[]{:S(2)}) collective-permute-start(f32[4,8,512]{2,1,0:T(8,128)S(1)} %bitcast.101), channel_id=1, source_target_pairs={{0,4},{4,0},{8,12},{12,8},{16,20},{20,16},{24,28},{28,24},{1,5},{5... | collective-permute-start | bytes 196616 | tf_op jit(solution)/shard_map/ppermute | solution.py:114

commit v2 on v1

v2 whole, which is shorter than its diff:
```python
import functools

import jax
import jax.numpy as jnp
from jax import lax
from jax.experimental import pallas as pl
from jax.experimental.pallas import tpu as pltpu
from jax.sharding import PartitionSpec as P

BINS = 256
LEVELS = 4095.0
LIGHT = (0.48, 0.6, 0.64)
GROUP = 8
CHUNKS = ((0, 4), (4, 6), (6, 9), (9, 10))
READY = ((0, 0), (0, 2), (2, 5), (5, 8))
EXT = GROUP + 2
MESH = pl.DeviceIdType.MESH


def planes(ext, right, left, k, c):
    def tile(step):
        at = lax.rem(c + 2 + step, EXT)
        lane = lax.broadcasted_iota(jnp.int32, (8, 128), 1)
        edge = jnp.where(lane < 64, right[k, at], left[k, at])
        return jnp.concatenate([ext[k, at], edge], axis=1)

    lo, mid, hi = tile(0), tile(1), tile(2)
    width = lo.shape[-1]
    cols = width - 128
    smooth = lo + 2.0 * mid + hi
    differ = hi - lo
    s_left, s_right = pltpu.roll(smooth, 1, 1)[:, :cols], pltpu.roll(smooth, width - 1, 1)[:, :cols]
    d_left, d_right = pltpu.roll(differ, 1, 1)[:, :cols], pltpu.roll(differ, width - 1, 1)[:, :cols]
    a = s_left + 2.0 * smooth[:, :cols] + s_right
    b = d_left + 2.0 * differ[:, :cols] + d_right
    g = s_right - s_left
    return a, b, g


def lookup(tables, voxels):
    outs = [[] for _ in range(4)]
    for j in range(voxels.shape[1] // 128):
        v = voxels[:, j * 128 : (j + 1) * 128]
        scaled = v * 17.0
        lower = jnp.floor((scaled + 0.5) * (1.0 / 273.0))
        fraction = (scaled - lower * 273.0) * (1.0 / 273.0)
        index = lower.astype(jnp.int32)
        high = index >= 128
        lane = jnp.bitwise_and(index, 127)
        for q in range(4):
            base = jnp.where(
                high,
                jnp.take_along_axis(tables[q][1], lane, axis=1),
                jnp.take_along_axis(tables[q][0], lane, axis=1),
            )
            step = jnp.where(
                high,
                jnp.take_along_axis(tables[q + 4][1], lane, axis=1),
                jnp.take_along_axis(tables[q + 4][0], lane, axis=1),
            )
            outs[q].append(base + fraction * step)
    return [jnp.concatenate(o, axis=1) for o in outs]


def load_tables(tab_ref):
    return [
        [jnp.broadcast_to(tab_ref[q : q + 1, h * 128 : (h + 1) * 128], (8, 128)) for h in range(2)]
        for q in range(8)
    ]


def blend(ascending, acc, new):
    trans = 1.0 - jnp.where(ascending, acc[3], new[3])
    return [
        jnp.where(ascending, a, n) + trans * jnp.where(ascending, n, a) for a, n in zip(acc, new)
    ]


def composite_tile(ext, right, left, tab_ref, ascending, c, slices):
    tables = load_tables(tab_ref)
    before = planes(ext, right, left, 0, c)
    here = planes(ext, right, left, 1, c)
    acc = None
    for k in range(1, slices + 1):
        after = planes(ext, right, left, k + 1, c)
        gd = after[0] - before[0]
        gr = before[1] + 2.0 * here[1] + after[1]
        gc = before[2] + 2.0 * here[2] + after[2]
        facing = LIGHT[0] * gd + LIGHT[1] * gr + LIGHT[2] * gc
        magnitude = gd * gd + gr * gr + gc * gc
        shading = 0.2 + 0.8 * jnp.abs(facing) * lax.rsqrt(magnitude + LEVELS * LEVELS)
        red, green, blue, opacity = lookup(tables, ext[k, lax.rem(c + 3, EXT)])
        weight = shading * opacity
        new = [red * weight, green * weight, blue * weight, opacity]
        acc = new if acc is None else blend(ascending, acc, new)
        before, here = here, after
    return acc


def render_kernel(
    nd, nc, vox, tab_ref, out_ref, rows_pad, ext, right, left, sent, sent_rows, got_rows,
    part, inbox, last_out, last_in, x_send, x_recv, h_send, h_recv,
    p_send, p_recv, f_send, f_recv,
):
    slices, rows, cols = vox.shape
    half = rows // 2
    d, col = lax.axis_index("depth"), lax.axis_index("col")
    x = lax.rem(d, 2)
    z = lax.rem(d, GROUP) // 2
    base = d - lax.rem(d, GROUP)
    odd = x == 1
    partner = d + 1 - 2 * x
    own = 1 + slices * x
    other = 1 + slices * (1 - x)
    first_k, last_k, end_k = 1, 2 * slices, 2 * slices + 1
    near_k = first_k + (last_k - first_k) * x
    far_k = last_k + (first_k - last_k) * x
    near_d = d - 2 + 4 * x
    far_d = d + 2 - 4 * x
    near_dst = end_k - end_k * x
    far_dst = end_k * x
    near_ok = jnp.logical_and(near_d >= 0, near_d < nd)
    far_ok = jnp.logical_and(far_d >= 0, far_d < nd)
    left_ok, right_ok = col > 0, col < nc - 1
    both = jnp.logical_and

    barrier = pltpu.get_barrier_semaphore()

    def greet(device, column, ok):
        @pl.when(ok)
        def _():
            pl.semaphore_signal(barrier, inc=1, device_id=(device, column), device_id_type=MESH)

        return jnp.where(ok, 1, 0)

    count = greet(partner, col, d >= 0)
    for step, ok in ((-1, left_ok), (1, right_ok)):
        count += greet(d, col + step, ok)
    for device, ok in ((near_d, near_ok), (far_d, far_ok)):
        count += greet(device, col, ok)
        for step, side in ((-1, left_ok), (1, right_ok)):
            count += greet(device, col + step, both(ok, side))
    for j in range(GROUP // 2):
        count += greet(base + 2 * j + x, col, z != j)

    pad = jnp.zeros((8, 128), jnp.float32)
    blocks = cols // 128

    def convert(k, carry):
        for j in range(blocks):
            lanes = slice(j * 128, j * 128 + 128)
            rows_pad[k, j, 0:8] = pad
            rows_pad[k, j, rows + 8 : rows + 16] = pad
            rows_pad[k, j, 8 : rows + 8] = vox[k, :, lanes].astype(jnp.float32)
            for c in range(EXT):
                at = (c + 2) % EXT
                upper = rows_pad[k, j, pl.ds(7 + c, 8, stride=8), :]
                lower = rows_pad[k, j, pl.ds(7 + c + half, 8, stride=8), :]
                ext[own + k, at, :, lanes] = jnp.where(odd, lower, upper)
                if 0 < c < EXT - 1:
                    sent[k, at, :, lanes] = jnp.where(odd, upper, lower)
        return carry

    lax.fori_loop(0, slices, convert, 0)
    for k in range(slices):
        for spot, up, low in ((k, 7, 7 + half), (slices + k, 8 + half, 8 + rows)):
            for j in range(blocks):
                sent_rows[spot : spot + 1, j * 128 : j * 128 + 128] = jnp.where(
                    odd, rows_pad[k, j, up : up + 1, :], rows_pad[k, j, low : low + 1, :]
                )

    def clear(ref, k):
        def one(i, carry):
            ref[k, i] = jnp.zeros(ref.shape[2:], jnp.float32)
            return carry

        lax.fori_loop(0, EXT, one, 0)

    for ok, k in ((far_ok, near_dst), (near_ok, far_dst)):
        @pl.when(jnp.logical_not(ok))
        def _(k=k):
            for ref in (ext, right, left):
                clear(ref, k)
    for ref, ok in ((right, right_ok), (left, left_ok)):
        @pl.when(jnp.logical_not(ok))
        def _(ref=ref):
            def every(k, carry):
                clear(ref, k)
                return carry

            lax.fori_loop(0, end_k + 1, every, 0)

    def remote(src, dst, ssem, rsem, device, column):
        return pltpu.make_async_remote_copy(
            src_ref=src, dst_ref=dst, send_sem=ssem, recv_sem=rsem,
            device_id=(device, column), device_id_type=MESH,
        )

    def halo_copies(h, start, k, dst, device, to_ok, from_ok, a, b):
        span = pl.ds(a, b - a)
        four = pl.ds(start, slices)
        first, last = pl.ds(0, 128), pl.ds(cols - 128, 128)
        entries = [
            (ext.at[k, span], ext.at[dst, span], device, col, to_ok, from_ok),
            (ext.at[four, span, :, first], right.at[four, span], d, col - 1, left_ok, right_ok),
            (ext.at[four, span, :, last], left.at[four, span], d, col + 1, right_ok, left_ok),
            (ext.at[k, span, :, first], right.at[dst, span], device, col - 1,
             both(to_ok, left_ok), both(from_ok, right_ok)),
            (ext.at[k, span, :, last], left.at[dst, span], device, col + 1,
             both(to_ok, right_ok), both(from_ok, left_ok)),
        ]
        return [
            (remote(s, t, h_send.at[h, i], h_recv.at[h, i], device, column), to, fr)
            for i, (s, t, device, column, to, fr) in enumerate(entries)
        ]

    def start_all(entries):
        for copy, to, _ in entries:
            pl.when(to)(copy.start)

    def receive_all(entries):
        for copy, _, fr in entries:
            pl.when(fr)(copy.wait_recv)

    pl.semaphore_wait(barrier, count)

    x_groups, number = [], 0
    for q, (lo, hi) in enumerate(CHUNKS):
        group = []
        for a, b in ((0, 1), (3, 4)) if q == 0 else ((lo, hi),):
            span = pl.ds(a, b - a)
            group.append(remote(
                sent.at[:, span], ext.at[pl.ds(own, slices), span],
                x_send.at[number], x_recv.at[number], partner, col,
            ))
            number += 1
        x_groups.append(group)
    x_groups[0].append(
        remote(sent_rows, got_rows, x_send.at[number], x_recv.at[number], partner, col)
    )
    whole = halo_copies(0, own, near_k, near_dst, near_d, near_ok, far_ok, 0, EXT)
    for copy in x_groups[0]:
        copy.start()
    start_all(whole)
    for group in x_groups[1:]:
        for copy in group:
            copy.start()

    ascending = jnp.broadcast_to(tab_ref[8:9, 0:1], (8, cols)) > 0.5
    row = lax.broadcasted_iota(jnp.int32, (8, cols), 0)

    def to_device(c):
        j, parity = c // 2, lax.rem(c, 2)
        return remote(
            part.at[c], inbox.at[parity, z], p_send.at[c], p_recv.at[parity, z],
            base + 2 * j + x, col,
        )

    def render(c, carry):
        acc = composite_tile(ext, right, left, tab_ref, ascending, c, 2 * slices)
        mine = c // 2 == z

        @pl.when(mine)
        def _():
            for i in range(4):
                inbox[lax.rem(c, 2), z, i] = acc[i]

        @pl.when(jnp.logical_not(mine))
        def _():
            for i in range(4):
                part[c, i] = acc[i]
            to_device(c).start()

        return carry

    forwards = []
    for q, (lo, hi) in enumerate(CHUNKS):
        for copy in x_groups[q]:
            copy.wait_recv()
        if q == 0:
            for k in range(slices):
                above = pltpu.roll(ext[other + k, 0], 1, 0)
                below = pltpu.roll(ext[other + k, 3], 7, 0)
                ext[other + k, 2] = jnp.where(row == 0, got_rows[k : k + 1, :], above)
                ext[other + k, 1] = jnp.where(
                    row == 7, got_rows[slices + k : slices + k + 1, :], below
                )
        ahead = halo_copies(1 + q, other, far_k, far_dst, far_d, far_ok, near_ok, lo, hi)
        start_all(ahead)
        forwards.append(ahead)
        if q == 0:
            receive_all(whole)
        else:
            receive_all(forwards[q - 1])
            lax.fori_loop(*READY[q - 1], render, 0)
    receive_all(forwards[-1])
    lax.fori_loop(*READY[-1], render, 0)

    def gathered(parity):
        for j in range(GROUP // 2):
            @pl.when(z != j)
            def _(j=j):
                remote(
                    part.at[0], inbox.at[parity, j], p_send.at[0], p_recv.at[parity, j],
                    partner, col,
                ).wait_recv()
        acc = None
        for j in range(GROUP // 2):
            new = [inbox[parity, j, i] for i in range(4)]
            acc = new if acc is None else blend(ascending, acc, new)
        return acc

    for i, value in enumerate(gathered(1 - x)):
        last_out[i] = value
    last = remote(last_out, last_in, f_send, f_recv, partner, col)
    last.start()
    for i, value in enumerate(gathered(x)):
        out_ref[i, pl.ds(pl.multiple_of(8 * x, 8), 8), :] = value
    last.wait_recv()
    for i in range(4):
        out_ref[i, pl.ds(pl.multiple_of(8 - 8 * x, 8), 8), :] = last_in[i]

    last.wait_send()
    for group in x_groups:
        for copy in group:
            copy.wait_send()
    for entries in [whole] + forwards:
        for copy, to, _ in entries:
            pl.when(to)(copy.wait_send)

    def drain(c, carry):
        @pl.when(c // 2 != z)
        def _():
            to_device(c).wait_send()

        return carry

    lax.fori_loop(0, GROUP, drain, 0)


def build_tables(color_table, opacity_table, brick_order):
    lower = jnp.concatenate([color_table, opacity_table[None]], axis=0).astype(jnp.float32)
    upper = jnp.concatenate([lower[:, 1:], lower[:, -1:]], axis=1)
    asc = (brick_order[0] < brick_order[-1]).astype(jnp.float32)
    return jnp.concatenate(
        [lower, upper - lower, jnp.full((8, BINS), asc, jnp.float32)], axis=0
    )


def swap(x, bit):
    return lax.ppermute(x, "depth", [(i, i ^ bit) for i in range(lax.axis_size("depth"))])


def over(front, back, axis):
    alpha = lax.slice_in_dim(front, 3, 4, axis=axis)
    return front + (1.0 - alpha) * back


def body(voxel_bins, color_table, opacity_table, brick_order):
    me = lax.axis_index("depth")
    n = lax.axis_size("depth")
    slices, rows, cols = voxel_bins.shape
    tiles = rows // GROUP
    tab = build_tables(color_table, opacity_table, brick_order)
    depth = 2 * slices + 2
    vmem = lambda *shape: pltpu.VMEM(shape, jnp.float32)
    dma = lambda *shape: pltpu.SemaphoreType.DMA(shape)
    chunks = len(CHUNKS)
    picture = pl.pallas_call(
        functools.partial(render_kernel, n, lax.axis_size("col")),
        out_shape=jax.ShapeDtypeStruct((4, tiles, cols), jnp.float32),
        in_specs=[pl.BlockSpec(memory_space=pltpu.VMEM)] * 2,
        out_specs=pl.BlockSpec(memory_space=pltpu.VMEM),
        scratch_shapes=[
            vmem(slices, cols // 128, rows + 16, 128),
            vmem(depth, EXT, 8, cols),
            vmem(depth, EXT, 8, 128),
            vmem(depth, EXT, 8, 128),
            vmem(slices, EXT, 8, cols),
            vmem(2 * slices, cols),
            vmem(2 * slices, cols),
            vmem(GROUP, 4, 8, cols),
            vmem(2, GROUP // 2, 4, 8, cols),
            vmem(4, 8, cols),
            vmem(4, 8, cols),
            dma(chunks + 2),
            dma(chunks + 2),
            dma(chunks + 1, 5),
            dma(chunks + 1, 5),
            dma(GROUP),
            dma(2, GROUP // 2),
            pltpu.SemaphoreType.DMA,
            pltpu.SemaphoreType.DMA,
        ],
        compiler_params=pltpu.CompilerParams(
            collective_id=0, has_side_effects=True, vmem_limit_bytes=40 * 2**20
        ),
    )(voxel_bins, tab)
    ascending = brick_order[0] < brick_order[-1]
    return finish(picture, ascending, me, n)


def finish(picture, ascending, me, n):
    bit = GROUP
    while bit < n:
        count = picture.shape[1]
        halves = picture.reshape(4, count // 2, 2, picture.shape[2])
        set_bit = me // bit % 2 == 1
        keep = jnp.where(set_bit, halves[:, :, 1], halves[:, :, 0])
        got = swap(jnp.where(set_bit, halves[:, :, 0], halves[:, :, 1]), bit)
        picture = jnp.where(set_bit != ascending, over(keep, got, 0), over(got, keep, 0))
        bit *= 2
    return picture[:, :, None, :]


def solution(mesh):
    in_specs = (P("depth", None, "col"), P(), P(), P())
    out_specs = P(None, None, "depth", "col")
    return jax.shard_map(body, mesh=mesh, in_specs=in_specs, out_specs=out_specs, check_vma=False)
```

time: 72.1 us -> 46.5 us (0.64)
  waiting for transfers between devices: 37.7 us -> 0 us
  Pallas kernels: 7.6 us -> 40.4 us
  starting transfers between devices: 13.2 us -> 0 us
  other arithmetic: 4.44 us -> 0.16 us
  local copies, waits for them, and re-layouts: 7.15 us -> 4.09 us
    ppermute x8 -> x0, waiting for transfers between devices: 37.7 us -> none  [the longest x4 29.3 us: swap(): lax.ppermute(x, 'depth', [(i, i ^ bit) for i in range(lax.axis_size('dept...]
    pallas_call x1, Pallas kernels: 7.6 us -> 40.4 us  [body(): pl.pallas_call(functools.partial(render_kernel, n, lax.axis_size('col')),...]
    ppermute x8 -> x0, starting transfers between devices: 13.2 us -> none  [the longest x4 3.94 us: swap(): lax.ppermute(x, 'depth', [(i, i ^ bit) for i in range(lax.axis_size('dept...]
    slice x14 -> x1, local copies, waits for them, and re-layouts: 4.42 us -> 0.58 us  [build_tables(): asc = (brick_order[0] < brick_order[-1]).astype(jnp.float32)]
    select_n x8 -> x0, other arithmetic: 2.21 us -> none  [the longest x1 0.79 us: body(): jnp.where(odd, jnp.concatenate([got, keep], axis=1), jnp.concatenate([kee...]
    convert_element_type x1 -> x0, other arithmetic: 1.32 us -> none  [body(): v = voxel_bins.astype(jnp.float32)]
    broadcast_in_dim x0 -> x1, local copies, waits for them, and re-layouts: none -> 0.79 us  [finish(): return picture[:, :, None, :]]
    unnamed x18 -> x6, local copies, waits for them, and re-layouts: 2.04 us -> 1.82 us
  transfers between devices with their start and end apart: 8 -> 0, of which waited for: 8 -> 0; matrix products, arithmetic and copies ran while one was open for 1% -> 0% of each run, Pallas kernels for 0% -> 0%
where the time goes in v2:
time: 46.5 us; the launch traced here: 46 us
  Pallas kernels  40.4 us (87%)
  local copies, waits for them, and re-layouts  4.09 us (9%)
  between operations  1.29 us (3%)
    pallas_call x1, Pallas kernels, body(): pl.pallas_call(functools.partial(render_kernel, n, lax.axis_size('col')),...  40.4 us
    unnamed x6, local copies, waits for them, and re-layouts  1.82 us

profile of v2, /device:TPU:28, one launch (start us, length us, event | category | flops | bytes accessed | tf_op | source)
XLA Modules:
  0.0 46.0 jit_solution(6446747563582852669)
XLA Ops:
  0.0 0.0 copy-start.2
  0.0 0.7 %broadcast_in_dim.9 = bf16[1,256]{1,0:T(2,128)(2,1)S(1)} reshape(bf16[256]{0:T(256)(128)(2,1)} %param.6) | data formatting | bytes 1024 | tf_op jit(solution)/shard_map/broadcast_in_dim | solution.py:342
  0.7 0.0 copy-done.2
  0.7 0.6 %fusion = (s32[1]{0:T(128)}, s32[1]{0:T(128)}) fusion(s32[8]{0:T(128)S(1)} %copy-done.2), kind=kLoop, calls=%fused_computation.3 | loop fusion | bytes 16 | tf_op jit(solution)/shard_map/slice | solution.py:344
  2.5 0.0 copy-start.1
  2.5 0.1 pad.2.clone
  2.6 0.6 %copy-done.1 = bf16[3,256]{1,0:T(4,128)(2,1)S(1)} copy-done((bf16[3,256]{1,0:T(4,128)(2,1)S(1)}, bf16[3,256]{1,0:T(4,128)(2,1)}, u32[]{:S(2)}) %copy-start.1) | copy-done | bytes 1560
  3.2 0.1 slice.17
  3.3 0.1 slice.16
  3.4 0.1 maximum_subtract_fusion
  3.4 0.1 maximum_maximum_fusion.tab_ref
  3.5 0.0 copy-start
  3.5 1.2 %copy-done = s32[4,128,512]{2,1,0:T(8,128)S(1)} copy-done((s32[4,128,512]{2,1,0:T(8,128)S(1)}, s32[4,128,512]{2,1,0:T(8,128)}, u32[]{:S(2)}) %copy-start) | copy-done | bytes 1048600
  4.7 40.4 %shard_map.46 = f32[4,16,512]{2,1,0:T(8,128)S(1)} custom-call(s32[4,128,512]{2,1,0:T(8,128)S(1)} %copy-done, f32[16,256]{1,0:T(8,128)S(1)} %maximum_maximum_fusion.tab_ref), custom_call_target="tpu_custom_call" | custom-call | tf_op jit(solution)/shard_map/pallas_call | solution.py:369
  45.2 0.8 %copy.5 = f32[4,16,1,512]{3,2,1,0:T(1,128)} copy(f32[4,16,1,512]{3,1,0,2:T(8,128)S(1)} %bitcast.2) | data formatting | bytes 262144 | tf_op jit(solution)/shard_map/broadcast_in_dim | solution.py:413
  (2 shorter events, 0.0 us)
Async XLA Ops:
  0.0 0.7 %copy-start.2 = (s32[8]{0:T(128)S(1)}, s32[8]{0:T(128)}, u32[]{:S(2)}) copy-start(s32[8]{0:T(128)} %param.7) | copy-start | bytes 100
  2.5 0.7 %copy-start.1 = (bf16[3,256]{1,0:T(4,128)(2,1)S(1)}, bf16[3,256]{1,0:T(4,128)(2,1)}, u32[]{:S(2)}) copy-start(bf16[3,256]{1,0:T(4,128)(2,1)} %param.5) | copy-start | bytes 4612
  3.5 1.2 %copy-start = (s32[4,128,512]{2,1,0:T(8,128)S(1)}, s32[4,128,512]{2,1,0:T(8,128)}, u32[]{:S(2)}) copy-start(s32[4,128,512]{2,1,0:T(8,128)} %vox.1) | copy-start | bytes 3145732

commit v3 on v2

--- a/solution.py
+++ b/solution.py
@@ -11,18 +11,15 @@
 LEVELS = 4095.0
 LIGHT = (0.48, 0.6, 0.64)
 GROUP = 8
-CHUNKS = ((0, 4), (4, 6), (6, 9), (9, 10))
-READY = ((0, 0), (0, 2), (2, 5), (5, 8))
+CHUNKS = GROUP - 1
 EXT = GROUP + 2
 MESH = pl.DeviceIdType.MESH
 
 
-def planes(ext, right, left, k, c):
+def planes(ext, edges, k, c):
     def tile(step):
         at = lax.rem(c + 2 + step, EXT)
-        lane = lax.broadcasted_iota(jnp.int32, (8, 128), 1)
-        edge = jnp.where(lane < 64, right[k, at], left[k, at])
-        return jnp.concatenate([ext[k, at], edge], axis=1)
+        return jnp.concatenate([ext[k, at], edges[k, at]], axis=1)
 
     lo, mid, hi = tile(0), tile(1), tile(2)
     width = lo.shape[-1]
@@ -76,13 +73,13 @@
     ]
 
 
-def composite_tile(ext, right, left, tab_ref, ascending, c, slices):
+def composite_tile(ext, edges, tab_ref, ascending, c, slices):
     tables = load_tables(tab_ref)
-    before = planes(ext, right, left, 0, c)
-    here = planes(ext, right, left, 1, c)
+    before = planes(ext, edges, 0, c)
+    here = planes(ext, edges, 1, c)
     acc = None
     for k in range(1, slices + 1):
-        after = planes(ext, right, left, k + 1, c)
+        after = planes(ext, edges, k + 1, c)
         gd = after[0] - before[0]
         gr = before[1] + 2.0 * here[1] + after[1]
         gc = before[2] + 2.0 * here[2] + after[2]
@@ -98,8 +95,9 @@
 
 
 def render_kernel(
-    nd, nc, vox, tab_ref, out_ref, rows_pad, ext, right, left, sent, sent_rows, got_rows,
-    part, inbox, last_out, last_in, x_send, x_recv, h_send, h_recv,
+    nd, nc, vox_hbm, color, opacity, order, out_ref, vox, tab_ref, rows_pad, ext, halos, edges,
+    own_edges, from_right, from_left, sent_edges, sent, sent_rows, got_rows,
+    part, inbox, last_out, last_in, v_sem, x_send, x_recv, h_send, h_recv, c_send, c_recv,
     p_send, p_recv, f_send, f_recv,
 ):
     slices, rows, cols = vox.shape
@@ -122,8 +120,12 @@
     near_ok = jnp.logical_and(near_d >= 0, near_d < nd)
     far_ok = jnp.logical_and(far_d >= 0, far_d < nd)
     left_ok, right_ok = col > 0, col < nc - 1
-    both = jnp.logical_and
-
+
+    loads = [
+        pltpu.make_async_copy(vox_hbm.at[k], vox.at[k], v_sem.at[k]) for k in range(slices)
+    ]
+    for load in loads:
+        load.start()
     barrier = pltpu.get_barrier_semaphore()
 
     def greet(device, column, ok):
@@ -138,15 +140,26 @@
         count += greet(d, col + step, ok)
     for device, ok in ((near_d, near_ok), (far_d, far_ok)):
         count += greet(device, col, ok)
-        for step, side in ((-1, left_ok), (1, right_ok)):
-            count += greet(device, col + step, both(ok, side))
     for j in range(GROUP // 2):
         count += greet(base + 2 * j + x, col, z != j)
 
     pad = jnp.zeros((8, 128), jnp.float32)
     blocks = cols // 128
 
-    def convert(k, carry):
+    lower_table = jnp.concatenate(
+        [color[...].astype(jnp.float32), opacity[...].astype(jnp.float32)], axis=0
+    )
+    bins = lower_table.shape[1]
+    entry = lax.broadcasted_iota(jnp.int32, (4, bins), 1)
+    upper_table = jnp.where(
+        entry == bins - 1, lower_table, jnp.concatenate([lower_table[:, 1:], lower_table[:, :1]], 1)
+    )
+    tab_ref[0:4] = lower_table
+    tab_ref[4:8] = upper_table - lower_table
+    lane = lax.broadcasted_iota(jnp.int32, (8, 128), 1)
+
+    def convert(k):
+        pack, pack_sent = pad, pad
         for j in range(blocks):
             lanes = slice(j * 128, j * 128 + 128)
             rows_pad[k, j, 0:8] = pad
@@ -157,11 +170,20 @@
                 upper = rows_pad[k, j, pl.ds(7 + c, 8, stride=8), :]
                 lower = rows_pad[k, j, pl.ds(7 + c + half, 8, stride=8), :]
                 ext[own + k, at, :, lanes] = jnp.where(odd, lower, upper)
+                here = jnp.where(odd, lower, upper)
+                there = jnp.where(odd, upper, lower)
+                for spot, block in ((2 * at, 0), ((2 * at + 127) % 128, blocks - 1)):
+                    if j == block:
+                        pack = jnp.where(lane == spot, pltpu.roll(here, 2 * at, 1), pack)
+                        pack_sent = jnp.where(lane == spot, pltpu.roll(there, 2 * at, 1), pack_sent)
                 if 0 < c < EXT - 1:
                     sent[k, at, :, lanes] = jnp.where(odd, upper, lower)
-        return carry
-
-    lax.fori_loop(0, slices, convert, 0)
+        own_edges[k] = pack
+        own_edges[slices + k] = pack_sent
+
+    for k in range(slices):
+        loads[k].wait()
+        convert(k)
     for k in range(slices):
         for spot, up, low in ((k, 7, 7 + half), (slices + k, 8 + half, 8 + rows)):
             for j in range(blocks):
@@ -179,16 +201,12 @@
     for ok, k in ((far_ok, near_dst), (near_ok, far_dst)):
         @pl.when(jnp.logical_not(ok))
         def _(k=k):
-            for ref in (ext, right, left):
-                clear(ref, k)
-    for ref, ok in ((right, right_ok), (left, left_ok)):
+            clear(ext, k)
+            edges[k] = pad
+    for ref, ok in ((from_right, right_ok), (from_left, left_ok)):
         @pl.when(jnp.logical_not(ok))
         def _(ref=ref):
-            def every(k, carry):
-                clear(ref, k)
-                return carry
-
-            lax.fori_loop(0, end_k + 1, every, 0)
+            ref[...] = jnp.zeros(ref.shape, jnp.float32)
 
     def remote(src, dst, ssem, rsem, device, column):
         return pltpu.make_async_remote_copy(
@@ -196,57 +214,81 @@
             device_id=(device, column), device_id_type=MESH,
         )
 
-    def halo_copies(h, start, k, dst, device, to_ok, from_ok, a, b):
-        span = pl.ds(a, b - a)
-        four = pl.ds(start, slices)
-        first, last = pl.ds(0, 128), pl.ds(cols - 128, 128)
-        entries = [
-            (ext.at[k, span], ext.at[dst, span], device, col, to_ok, from_ok),
-            (ext.at[four, span, :, first], right.at[four, span], d, col - 1, left_ok, right_ok),
-            (ext.at[four, span, :, last], left.at[four, span], d, col + 1, right_ok, left_ok),
-            (ext.at[k, span, :, first], right.at[dst, span], device, col - 1,
-             both(to_ok, left_ok), both(from_ok, right_ok)),
-            (ext.at[k, span, :, last], left.at[dst, span], device, col + 1,
-             both(to_ok, right_ok), both(from_ok, left_ok)),
-        ]
-        return [
-            (remote(s, t, h_send.at[h, i], h_recv.at[h, i], device, column), to, fr)
-            for i, (s, t, device, column, to, fr) in enumerate(entries)
-        ]
-
-    def start_all(entries):
-        for copy, to, _ in entries:
-            pl.when(to)(copy.start)
-
-    def receive_all(entries):
-        for copy, _, fr in entries:
-            pl.when(fr)(copy.wait_recv)
+    def tile_of(q):
+        return jnp.where(lax.rem(q, 2) == 1, (q + 1) // 2, GROUP - 1 - q // 2)
+
+    def x_copy(q):
+        span = pl.ds(tile_of(q) + 3, 1)
+        return remote(
+            sent.at[:, span], ext.at[pl.ds(own, slices), span],
+            x_send.at[q], x_recv.at[q], partner, col,
+        )
+
+    def far_copy(q):
+        span = pl.ds(tile_of(q) + 3, 1)
+        return remote(
+            ext.at[far_k, span], ext.at[far_dst, span],
+            h_send.at[q], h_recv.at[q], far_d, col,
+        )
+
+    first_x = [
+        remote(
+            sent.at[:, pl.ds(at, 1)], ext.at[pl.ds(own, slices), pl.ds(at, 1)],
+            x_send.at[i], x_recv.at[i], partner, col,
+        )
+        for i, at in ((0, 0), (CHUNKS, 3))
+    ]
+    first_x.append(
+        remote(sent_rows, got_rows, x_send.at[CHUNKS + 1], x_recv.at[CHUNKS + 1], partner, col)
+    )
+    edge_x = remote(
+        sent_edges, edges.at[pl.ds(own, slices)],
+        x_send.at[CHUNKS + 2], x_recv.at[CHUNKS + 2], partner, col,
+    )
+    to_left = remote(own_edges, from_right, c_send.at[0], c_recv.at[0], d, col - 1)
+    to_right = remote(own_edges, from_left, c_send.at[1], c_recv.at[1], d, col + 1)
+    near = remote(
+        ext.at[near_k], ext.at[near_dst], h_send.at[CHUNKS], h_recv.at[CHUNKS], near_d, col
+    )
+    near_edge = remote(
+        edges.at[near_k], edges.at[near_dst],
+        h_send.at[CHUNKS + 1], h_recv.at[CHUNKS + 1], near_d, col,
+    )
+    far_first = remote(
+        ext.at[far_k, pl.ds(0, 4)], ext.at[far_dst, pl.ds(0, 4)],
+        h_send.at[0], h_recv.at[0], far_d, col,
+    )
+    far_edge = remote(
+        edges.at[far_k], edges.at[far_dst],
+        h_send.at[CHUNKS + 2], h_recv.at[CHUNKS + 2], far_d, col,
+    )
 
     pl.semaphore_wait(barrier, count)
-
-    x_groups, number = [], 0
-    for q, (lo, hi) in enumerate(CHUNKS):
-        group = []
-        for a, b in ((0, 1), (3, 4)) if q == 0 else ((lo, hi),):
-            span = pl.ds(a, b - a)
-            group.append(remote(
-                sent.at[:, span], ext.at[pl.ds(own, slices), span],
-                x_send.at[number], x_recv.at[number], partner, col,
-            ))
-            number += 1
-        x_groups.append(group)
-    x_groups[0].append(
-        remote(sent_rows, got_rows, x_send.at[number], x_recv.at[number], partner, col)
-    )
-    whole = halo_copies(0, own, near_k, near_dst, near_d, near_ok, far_ok, 0, EXT)
-    for copy in x_groups[0]:
+    pl.when(left_ok)(to_left.start)
+    pl.when(right_ok)(to_right.start)
+    for copy in first_x:
         copy.start()
-    start_all(whole)
-    for group in x_groups[1:]:
-        for copy in group:
-            copy.start()
-
-    ascending = jnp.broadcast_to(tab_ref[8:9, 0:1], (8, cols)) > 0.5
+    x_copy(1).start()
+    pl.when(near_ok)(near.start)
+    pl.when(right_ok)(to_left.wait_recv)
+    pl.when(left_ok)(to_right.wait_recv)
+    for k in range(slices):
+        even = jnp.bitwise_and(lane, 1) == 0
+        edges[own + k] = jnp.where(even, from_right[k], from_left[k])
+        sent_edges[k] = jnp.where(even, from_right[slices + k], from_left[slices + k])
+    edge_x.start()
+    pl.when(near_ok)(near_edge.start)
+
+    def later(q, carry):
+        x_copy(q).start()
+        return carry
+
+    lax.fori_loop(2, CHUNKS, later, 0)
+
+    last_brick = order.shape[0] - 1
+    ascending = jnp.broadcast_to(
+        jnp.where(order[0] < order[last_brick], 1, 0), (8, cols)
+    ) == 1
     row = lax.broadcasted_iota(jnp.int32, (8, cols), 0)
 
     def to_device(c):
@@ -256,8 +298,21 @@
             base + 2 * j + x, col,
         )
 
-    def render(c, carry):
-        acc = composite_tile(ext, right, left, tab_ref, ascending, c, 2 * slices)
+    def render(i, carry):
+        @pl.when(i + 2 < CHUNKS)
+        def _():
+            x_copy(i + 2).wait_recv()
+
+            @pl.when(far_ok)
+            def _():
+                far_copy(i + 2).start()
+
+        @pl.when(jnp.logical_and(i + 1 < CHUNKS, near_ok))
+        def _():
+            far_copy(i + 1).wait_recv()
+
+        c = jnp.where(lax.rem(i, 2) == 0, i // 2, GROUP - 1 - i // 2)
+        acc = composite_tile(ext, halos, tab_ref, ascending, c, 2 * slices)
         mine = c // 2 == z
 
         @pl.when(mine)
@@ -273,28 +328,31 @@
 
         return carry
 
-    forwards = []
-    for q, (lo, hi) in enumerate(CHUNKS):
-        for copy in x_groups[q]:
-            copy.wait_recv()
-        if q == 0:
-            for k in range(slices):
-                above = pltpu.roll(ext[other + k, 0], 1, 0)
-                below = pltpu.roll(ext[other + k, 3], 7, 0)
-                ext[other + k, 2] = jnp.where(row == 0, got_rows[k : k + 1, :], above)
-                ext[other + k, 1] = jnp.where(
-                    row == 7, got_rows[slices + k : slices + k + 1, :], below
-                )
-        ahead = halo_copies(1 + q, other, far_k, far_dst, far_d, far_ok, near_ok, lo, hi)
-        start_all(ahead)
-        forwards.append(ahead)
-        if q == 0:
-            receive_all(whole)
-        else:
-            receive_all(forwards[q - 1])
-            lax.fori_loop(*READY[q - 1], render, 0)
-    receive_all(forwards[-1])
-    lax.fori_loop(*READY[-1], render, 0)
+    for copy in first_x:
+        copy.wait_recv()
+    for k in range(slices):
+        above = pltpu.roll(ext[other + k, 0], 1, 0)
+        below = pltpu.roll(ext[other + k, 3], 7, 0)
+        ext[other + k, 2] = jnp.where(row == 0, got_rows[k : k + 1, :], above)
+        ext[other + k, 1] = jnp.where(row == 7, got_rows[slices + k : slices + k + 1, :], below)
+    pl.when(far_ok)(far_first.start)
+    x_copy(1).wait_recv()
+    pl.when(far_ok)(far_copy(1).start)
+    edge_x.wait_recv()
+    pl.when(far_ok)(far_edge.start)
+    pl.when(far_ok)(near.wait_recv)
+    pl.when(far_ok)(near_edge.wait_recv)
+    pl.when(near_ok)(far_first.wait_recv)
+    pl.when(near_ok)(far_edge.wait_recv)
+
+    def unpack(k, carry):
+        packed = edges[k]
+        for at in range(EXT):
+            halos[k, at] = pltpu.roll(packed, (128 - 2 * at) % 128, 1)
+        return carry
+
+    lax.fori_loop(0, end_k + 1, unpack, 0)
+    lax.fori_loop(0, GROUP, render, 0)
 
     def gathered(parity):
         for j in range(GROUP // 2):
@@ -321,12 +379,24 @@
         out_ref[i, pl.ds(pl.multiple_of(8 - 8 * x, 8), 8), :] = last_in[i]
 
     last.wait_send()
-    for group in x_groups:
-        for copy in group:
-            copy.wait_send()
-    for entries in [whole] + forwards:
-        for copy, to, _ in entries:
-            pl.when(to)(copy.wait_send)
+    for copy in first_x + [edge_x]:
+        copy.wait_send()
+    for copy, ok in (
+        (to_left, left_ok), (to_right, right_ok), (near, near_ok), (near_edge, near_ok),
+        (far_first, far_ok), (far_edge, far_ok),
+    ):
+        pl.when(ok)(copy.wait_send)
+
+    def drain_x(q, carry):
+        x_copy(q).wait_send()
+
+        @pl.when(far_ok)
+        def _():
+            far_copy(q).wait_send()
+
+        return carry
+
+    lax.fori_loop(1, CHUNKS, drain_x, 0)
 
     def drain(c, carry):
         @pl.when(c // 2 != z)
@@ -336,15 +406,6 @@
         return carry
 
     lax.fori_loop(0, GROUP, drain, 0)
-
-
-def build_tables(color_table, opacity_table, brick_order):
-    lower = jnp.concatenate([color_table, opacity_table[None]], axis=0).astype(jnp.float32)
-    upper = jnp.concatenate([lower[:, 1:], lower[:, -1:]], axis=1)
-    asc = (brick_order[0] < brick_order[-1]).astype(jnp.float32)
-    return jnp.concatenate(
-        [lower, upper - lower, jnp.full((8, BINS), asc, jnp.float32)], axis=0
-    )
 
 
 def swap(x, bit):
@@ -361,21 +422,30 @@
     n = lax.axis_size("depth")
     slices, rows, cols = voxel_bins.shape
     tiles = rows // GROUP
-    tab = build_tables(color_table, opacity_table, brick_order)
     depth = 2 * slices + 2
     vmem = lambda *shape: pltpu.VMEM(shape, jnp.float32)
     dma = lambda *shape: pltpu.SemaphoreType.DMA(shape)
-    chunks = len(CHUNKS)
     picture = pl.pallas_call(
         functools.partial(render_kernel, n, lax.axis_size("col")),
         out_shape=jax.ShapeDtypeStruct((4, tiles, cols), jnp.float32),
-        in_specs=[pl.BlockSpec(memory_space=pltpu.VMEM)] * 2,
+        in_specs=[
+            pl.BlockSpec(memory_space=pltpu.HBM),
+            pl.BlockSpec(memory_space=pltpu.VMEM),
+            pl.BlockSpec(memory_space=pltpu.VMEM),
+            pl.BlockSpec(memory_space=pltpu.SMEM),
+        ],
         out_specs=pl.BlockSpec(memory_space=pltpu.VMEM),
         scratch_shapes=[
+            pltpu.VMEM((slices, rows, cols), jnp.int32),
+            vmem(8, BINS),
             vmem(slices, cols // 128, rows + 16, 128),
             vmem(depth, EXT, 8, cols),
             vmem(depth, EXT, 8, 128),
-            vmem(depth, EXT, 8, 128),
+            vmem(depth, 8, 128),
+            vmem(2 * slices, 8, 128),
+            vmem(2 * slices, 8, 128),
+            vmem(2 * slices, 8, 128),
+            vmem(slices, 8, 128),
             vmem(slices, EXT, 8, cols),
             vmem(2 * slices, cols),
             vmem(2 * slices, cols),
@@ -383,10 +453,13 @@
             vmem(2, GROUP // 2, 4, 8, cols),
             vmem(4, 8, cols),
             vmem(4, 8, cols),
-            dma(chunks + 2),
-            dma(chunks + 2),
-            dma(chunks + 1, 5),
-            dma(chunks + 1, 5),
+            dma(slices),
+            dma(CHUNKS + 3),
+            dma(CHUNKS + 3),
+            dma(CHUNKS + 3),
+            dma(CHUNKS + 3),
+            dma(2),
+            dma(2),
             dma(GROUP),
             dma(2, GROUP // 2),
             pltpu.SemaphoreType.DMA,
@@ -395,7 +468,7 @@
         compiler_params=pltpu.CompilerParams(
             collective_id=0, has_side_effects=True, vmem_limit_bytes=40 * 2**20
         ),
-    )(voxel_bins, tab)
+    )(voxel_bins, color_table, opacity_table[None], brick_order)
     ascending = brick_order[0] < brick_order[-1]
     return finish(picture, ascending, me, n)
 

time: 46.5 us -> 40.5 us (0.87)
  the two profiles are of different devices: /device:TPU:28 before, /device:TPU:14 now
where the time goes in v3:
time: 40.5 us; the launch traced here: 40.3 us
  Pallas kernels  36.9 us (91%)
  local copies, waits for them, and re-layouts  3.37 us (8%)
    pallas_call x1, Pallas kernels, body(): pl.pallas_call(functools.partial(render_kernel, n, lax.axis_size('col')),...  36.9 us
    unnamed x6, local copies, waits for them, and re-layouts  1.91 us

profile of v3, /device:TPU:14, one launch (start us, length us, event | category | flops | bytes accessed | tf_op | source)
XLA Modules:
  0.0 40.3 jit_solution(18216600511250861475)
XLA Ops:
  0.0 0.0 copy-start.2
  0.0 0.7 %broadcast_in_dim.6.opacity = bf16[1,256]{1,0:T(2,128)(2,1)S(1)} reshape(bf16[256]{0:T(256)(128)(2,1)} %param.6) | data formatting | bytes 1024 | tf_op jit(solution)/shard_map/broadcast_in_dim | solution.py:471
  0.7 0.0 copy-done.2
  0.7 0.0 copy-start
  0.7 1.2 %copy-done = s32[4,128,512]{2,1,0:T(8,128)S(1)} copy-done((s32[4,128,512]{2,1,0:T(8,128)S(1)}, s32[4,128,512]{2,1,0:T(8,128)}, u32[]{:S(2)}) %copy-start) | copy-done | bytes 1048600
  1.9 0.0 copy-start.1
  1.9 0.7 %copy-done.1 = bf16[3,256]{1,0:T(4,128)(2,1)S(1)} copy-done((bf16[3,256]{1,0:T(4,128)(2,1)S(1)}, bf16[3,256]{1,0:T(4,128)(2,1)}, u32[]{:S(2)}) %copy-start.1) | copy-done | bytes 1560
  2.6 36.9 %shard_map.46 = f32[4,16,512]{2,1,0:T(8,128)S(1)} custom-call(s32[4,128,512]{2,1,0:T(8,128)S(1)} %copy-done, bf16[3,256]{1,0:T(4,128)(2,1)S(1)} %copy-done.1, bf16[1,256]{1,0:T(2,128)(2,1)S(1)} %broadcast_in_dim.6.opacity, s32[8]{0:T(128)S(1)} %copy-done.2), custom_call_target="tpu_custom_call" | custom-call | tf_op jit(solution)/shard_map/pallas_call | solution.py:428
  39.5 0.8 %copy.5 = f32[4,16,1,512]{3,2,1,0:T(1,128)} copy(f32[4,16,1,512]{3,1,0,2:T(8,128)S(1)} %bitcast.1) | data formatting | bytes 262144 | tf_op jit(solution)/shard_map/broadcast_in_dim | solution.py:486
Async XLA Ops:
  0.0 0.7 %copy-start.2 = (s32[8]{0:T(128)S(1)}, s32[8]{0:T(128)}, u32[]{:S(2)}) copy-start(s32[8]{0:T(128)} %order.1) | copy-start | bytes 100
  0.7 1.2 %copy-start = (s32[4,128,512]{2,1,0:T(8,128)S(1)}, s32[4,128,512]{2,1,0:T(8,128)}, u32[]{:S(2)}) copy-start(s32[4,128,512]{2,1,0:T(8,128)} %vox_hbm.1) | copy-start | bytes 3145732
  1.9 0.7 %copy-start.1 = (bf16[3,256]{1,0:T(4,128)(2,1)S(1)}, bf16[3,256]{1,0:T(4,128)(2,1)}, u32[]{:S(2)}) copy-start(bf16[3,256]{1,0:T(4,128)(2,1)} %color.1) | copy-start | bytes 4612
